TPU v7x, 256 devices: a whole 4x4x8 slice. The times are simulated.
256 devices in a mesh: ia: 8 (over z), ja: 8 (over y, core), ka: 4 (over x).
Axes of the slice: x: 4, y: 4, z: 8, core: 2. Of those that a mesh axis runs over, the one named last changes fastest.
Arguments:
- tensor: bfloat16 [4096, 64, 4096], P('ia', 'ka', 'ja'), may hold values from -6 to 6
- factor_b: float32 [4096, 32], P(('ja', 'ia')), may hold values from -1 to 1, as said below
- factor_c: float32 [64, 32], P('ka'), may hold values from -1 to 1, as said below
Outputs:
- factor_a: float32 [4096, 32], P(('ia', 'ja', 'ka'))
Inputs may be any that keep to these rules, and one draw needn't show every extreme that they name: `factor_b`: dense real entries; columns of different scales with a part common to all columns. `factor_c`: dense real entries; columns of different scales with a part common to all columns.
All inputs are finite; a program needn't handle non-finite values.
Results may differ from a plain program's by a relative error of at most 0.0041.
Values sent between devices are 32-bit elements; how exact they have to be, the bound alone decides.
A program may use at most 64 MiB of HBM per device.

v0:
```python
import jax
import jax.numpy as jnp
from jax import lax
from jax.sharding import PartitionSpec as P


def apply_inverse(matrix, lower_factor):
    return jax.scipy.linalg.solve_triangular(lower_factor, matrix.T, lower=True).T


def per_device(tensor, factor_b, factor_c):
    highest = lax.Precision.HIGHEST
    local_b = jnp.dot(factor_b.T, factor_b, precision=highest)
    local_c = jnp.dot(factor_c.T, factor_c, precision=highest)
    gram_b = lax.psum(local_b, ("ia", "ja"))
    gram_c = lax.psum(local_c, "ka")
    low_b = jnp.linalg.cholesky(gram_b)
    low_c = jnp.linalg.cholesky(gram_c)
    rows_b = lax.all_gather(factor_b, "ia", axis=0, tiled=True)
    q_b = apply_inverse(rows_b, low_b).astype(jnp.bfloat16)
    q_c = apply_inverse(factor_c, low_c).astype(jnp.bfloat16)
    block_i, block_k, block_j = tensor.shape
    rank = factor_b.shape[1]
    flat = jnp.dot(
        tensor.reshape(block_i * block_k, block_j), q_b, preferred_element_type=jnp.float32
    )
    flat = flat.reshape(block_i, block_k, rank)
    core = jnp.einsum("iks,kt->its", flat, q_c.astype(jnp.float32), precision=highest).reshape(
        block_i, rank * rank
    )
    kron_r = (low_c.T[:, None, :] * low_b.T[None, :, :]).reshape(rank * rank, rank)
    low_zero = jnp.linalg.cholesky(gram_c * gram_b)
    q_zero = apply_inverse(kron_r, low_zero)
    summed = lax.psum_scatter(core, ("ja", "ka"), scatter_dimension=0, tiled=True)
    projected = jnp.dot(summed, q_zero, precision=highest)
    return jax.scipy.linalg.solve_triangular(low_zero, projected.T, lower=True, trans=1).T


def solution(mesh):
    return jax.shard_map(
        per_device,
        mesh=mesh,
        in_specs=(P("ia", "ka", "ja"), P(("ja", "ia"), None), P("ka", None)),
        out_specs=P(("ia", "ja", "ka"), None),
        check_vma=False,
    )
```

profile of v0, /device:TPU:1, one launch (start us, length us, event | category | flops | bytes accessed | tf_op | source)
XLA Modules:
  0.0 420.4 jit_solution(442166573601847893)
XLA Ops:
  6.5 0.0 copy-start
  6.5 0.0 reduce-scatter.4.cloned.1.call-start
  6.5 0.9 fusion.14
  7.5 249.7 %psum.15 = f32[32,32]{0,1:T(8,128)S(1)} all-reduce(f32[32,32]{0,1:T(8,128)S(1)} %fusion.14), channel_id=1, replica_groups=mesh['ia'=8,'ja'=8,'ka'=4] {'ia','ja'}, use_global_device_ids=true, to_apply=%region_1.0 | all-reduce | flops 1024 | bytes 8192 | tf_op jit(solution)/shard_map/psum | solution.py:15
  257.2 0.1 copy.28
  257.3 2.9 cholesky.81
  260.2 0.6 compare_reduce_fusion
  260.9 0.7 select_bitcast_fusion
  261.5 2.4 custom-call.19
  264.0 0.0 copy-done
  264.0 0.2 fusion.13
  264.2 13.1 %psum.14 = f32[32,32]{0,1:T(8,128)S(1)} all-reduce(f32[32,32]{0,1:T(8,128)S(1)} %fusion.13), channel_id=1, replica_groups=mesh['ia'=8,'ja'=8,'ka'=4] {'ka'}, use_global_device_ids=true, to_apply=%region_0.0 | all-reduce | flops 1024 | bytes 8192 | tf_op jit(solution)/shard_map/psum | solution.py:16
  277.3 0.1 copy.26
  277.4 2.9 cholesky.70
  280.4 0.6 compare_reduce_fusion.1
  281.0 0.7 select_bitcast_fusion.1
  281.7 2.4 custom-call.18
  284.1 0.2 fusion
  284.3 18.4 %all-gather = f32[8,64,32]{1,2,0:T(8,128)S(1)} all-gather(f32[1,64,32]{1,2,0:T(8,128)} %bitcast.65), channel_id=1, replica_groups=mesh['ia'=8,'ja'=8,'ka'=4] {'ia'}, dimensions={0}, use_global_device_ids=true | all-gather | bytes 73728 | tf_op jit(solution)/shard_map/all_gather | solution.py:19
  302.7 0.1 copy.30
  302.8 0.1 reshape.48
  302.9 0.3 convolution_convert_fusion
  303.1 5.9 %convolution_bitcast_fusion = f32[8192,32]{0,1:T(8,128)S(1)} fusion(bf16[32,512]{1,0:T(8,128)(2,1)S(1)} %convolution_convert_fusion, bf16[8192,512]{1,0:T(8,128)(2,1)} %bitcast.61), kind=kOutput, calls=%fused_computation | convolution fusion | flops 268435456 | bytes 9469952 | tf_op jit(solution)/shard_map/dot_general | solution.py:24
  309.0 2.6 copy.31
  311.7 3.2 copy.32
  314.9 1.0 convolution_bitcast_fusion.1
  315.9 1.2 copy.33
  317.2 1.9 copy.36
  319.1 0.0 reduce-scatter.4.cloned.1.call-update
  319.1 0.1 copy.29
  319.2 0.1 copy.25
  319.2 2.9 cholesky.59
  322.2 0.6 compare_reduce_fusion.2
  322.8 0.7 fusion.1
  323.5 2.4 custom-call.17
  325.9 0.1 copy.27
  326.0 0.1 broadcast_multiply_fusion
  326.1 0.6 fusion.8
  326.7 85.0 %reduce-scatter.4.cloned.1.call-done = f32[16,1024]{1,0:T(8,128)} async-done(((f32[512,1024]{1,0:T(8,128)}), f32[16,1024]{1,0:T(8,128)}) %reduce-scatter.4.cloned.1.call-update) | async-done | bytes 65552
  411.7 1.0 fusion.15
  412.7 0.8 fusion.6
  (7 shorter events, 0.1 us)
Async XLA Ops:
  6.5 257.4 %copy-start = (f32[16,32]{1,0:T(8,128)S(1)}, f32[16,32]{1,0:T(8,128)}, u32[]{:S(2)}) copy-start(f32[16,32]{1,0:T(8,128)} %param.6) | copy-start | bytes 6148
  6.5 405.2 %reduce-scatter.4.cloned.1.call-start = ((), (), s32[]{:S(2)}) async-start(), calls=%async_computation.1 | async-start | bytes 2162688
Sparse Core Ops, SparseCore 0:
  319.2 92.4 reduce-scatter.3
where the time goes:
time: 421 us; the launch traced here: 420 us
  blocking collectives  281 us (67%)
  waiting for transfers between devices  85 us (20%)
  other arithmetic  20.2 us (5%)
  between operations  13.5 us (3%)
  matrix products  11 us (3%)
  local copies, waits for them, and re-layouts  9.5 us (2%)
    psum x1, blocking collectives, per_device(): gram_b = lax.psum(local_b, ('ia', 'ja'))  250 us
    unnamed x2, waiting for transfers between devices  85 us
    all_gather x1, blocking collectives, per_device(): rows_b = lax.all_gather(factor_b, 'ia', axis=0, tiled=True)  18.4 us
    psum x1, blocking collectives, per_device(): gram_c = lax.psum(local_c, 'ka')  13.1 us
  transfers between devices with their start and end apart: 1, of which 1 were waited for; matrix products, arithmetic and copies ran while one was open for 2% of the time, Pallas kernels for 0%

commit v1 on v0

v1 whole, which is shorter than its diff:
```python
import functools

import jax
import jax.numpy as jnp
from jax import lax
from jax.experimental import pallas as pl
from jax.experimental.pallas import tpu as pltpu
from jax.sharding import PartitionSpec as P

MESH = pl.DeviceIdType.MESH
HIGHEST = lax.Precision.HIGHEST
F32 = jnp.float32
BF16 = jnp.bfloat16
LANES = 128


def lane_group(shape, rank):
    return lax.broadcasted_iota(jnp.int32, shape, 1) // rank


def tile_lanes(x):
    return jnp.concatenate([x] * (LANES // x.shape[1]), axis=1)


def pack_rows(x, rank):
    groups = LANES // rank
    m = x.shape[0] // groups
    lane = lane_group((m, LANES), rank)
    packed = x[:m]
    for g in range(1, groups):
        packed = jnp.where(lane == g, x[g * m:(g + 1) * m], packed)
    return packed


def inverse_spd(matrix):
    n = matrix.shape[0]
    row_id = lax.broadcasted_iota(jnp.int32, (n, n), 0)
    lane_id = lax.broadcasted_iota(jnp.int32, (n, n), 1)
    lane_row = lax.broadcasted_iota(jnp.int32, (1, n), 1)
    for k in range(n):
        row = matrix[k:k + 1, :]
        col = matrix[:, k:k + 1]
        inv = 1.0 / matrix[k:k + 1, k:k + 1]
        scaled = jnp.where(lane_row == k, inv, row * inv)
        rest = jnp.where(lane_id == k, 0.0, matrix)
        matrix = jnp.where(row_id == k, scaled, rest - col * scaled)
    return matrix


def kernel(sizes, tensor_ref, fbt_ref, fc_ref, out_ref,
           tbuf, fbt_own, fc_own, fb_send, fb_all, gc_all, gb_all, weights, send, recv,
           load_sem, own_sem, fb_s, fb_r, gc_s, gc_r, gb_s, gb_r, m_s, m_r):
    n_ia, n_ja, n_ka = sizes
    ia, ja, ka = lax.axis_index("ia"), lax.axis_index("ja"), lax.axis_index("ka")
    rank, shard = fbt_own.shape
    block_k = tbuf.shape[1]
    block_j = tbuf.shape[2]
    rows = out_ref.shape[0]
    group_rows = rows * n_ka
    groups = LANES // rank

    def up(index, by, size):
        return lax.rem(index + by, size)

    own_b = pltpu.make_async_copy(fbt_ref, fbt_own, own_sem.at[0])
    own_c = pltpu.make_async_copy(fc_ref, fc_own, own_sem.at[1])
    own_b.start()
    own_c.start()

    def load(step):
        first = pl.multiple_of(up(ja, step + 1, n_ja) * group_rows, group_rows)
        part = pl.ds(first, group_rows)
        return pltpu.make_async_copy(tensor_ref.at[part], tbuf.at[part], load_sem.at[step])

    @pl.loop(0, n_ja)
    def _(step):
        load(step).start()

    barrier = pltpu.get_barrier_semaphore()

    @pl.loop(1, n_ia)
    def _(d):
        pl.semaphore_signal(barrier, inc=1, device_id={"ia": up(ia, d, n_ia)}, device_id_type=MESH)

    @pl.loop(1, n_ja * n_ka)
    def _(d):
        pl.semaphore_signal(barrier, inc=1, device_id={"ja": up(ja, d // n_ka, n_ja), "ka": up(ka, d % n_ka, n_ka)}, device_id_type=MESH)

    own_b.wait()
    own_c.wait()
    half = rank // 2
    own = fbt_own[...]
    packed_b = jnp.concatenate([own[:half], own[half:]], axis=1)
    fb_send[...] = packed_b
    fb_all[ia] = packed_b
    fc_tiled = tile_lanes(fc_own[...])
    gc_all[0] = pack_rows(
        lax.dot_general(fc_own[...], fc_tiled, (((0,), (0,)), ((), ())), precision=HIGHEST, preferred_element_type=F32), rank)
    pl.semaphore_wait(barrier, n_ia - 1 + n_ja * n_ka - 1)

    @pl.loop(1, n_ia)
    def _(d):
        pltpu.make_async_remote_copy(fb_send, fb_all.at[ia], fb_s, fb_r, device_id={"ia": up(ia, d, n_ia)}, device_id_type=MESH).start()

    @pl.loop(1, n_ka)
    def _(d):
        pltpu.make_async_remote_copy(gc_all.at[0], gc_all.at[n_ka - d], gc_s, gc_r, device_id={"ka": up(ka, d, n_ka)}, device_id_type=MESH).start()

    fb_part = fb_all.at[pl.ds(0, n_ia - 1)]
    pltpu.make_async_copy(fb_part, fb_part, fb_r).wait()

    uppers, lowers = [], []
    for s in range(n_ia):
        piece = fb_all[s]
        uppers.append(piece[:, :shard])
        lowers.append(piece[:, shard:])
    fbt = jnp.concatenate([jnp.concatenate(uppers, axis=1), jnp.concatenate(lowers, axis=1)], axis=0)
    high = fbt.astype(BF16)
    rest = fbt - high.astype(F32)
    middle = rest.astype(BF16)
    low = (rest - middle.astype(F32)).astype(BF16)
    stacked = jnp.concatenate([high.astype(F32), middle.astype(F32), low.astype(F32), jnp.zeros_like(fbt)], axis=0)
    weights[...] = stacked.T.astype(BF16)

    gb_all[0] = pack_rows(
        lax.dot_general(fbt, jnp.concatenate([fbt] * groups, axis=0), (((1,), (1,)), ((), ())), precision=HIGHEST, preferred_element_type=F32), rank)

    @pl.loop(1, n_ja)
    def _(d):
        pltpu.make_async_remote_copy(gb_all.at[0], gb_all.at[n_ja - d], gb_s, gb_r, device_id={"ja": up(ja, d, n_ja)}, device_id_type=MESH).start()

    def contract(step):
        load(step).wait()
        first = pl.multiple_of(up(ja, step + 1, n_ja) * group_rows, group_rows)
        x = tbuf[pl.ds(first, group_rows)].reshape(group_rows * block_k, block_j)
        flat = jnp.dot(x, weights[...], preferred_element_type=F32).reshape(group_rows, block_k, LANES)
        part = jnp.sum(flat * fc_tiled[None], axis=1)
        part = part + pltpu.roll(part, 2 * rank, 1)
        part = part + pltpu.roll(part, rank, 1)
        for b in range(n_ka):
            send[step * n_ka + b] = pack_rows(part[b * rows:(b + 1) * rows], rank)

    def push(step, dk):
        to_j, to_k = up(ja, step + 1, n_ja), up(ka, dk, n_ka)
        slot = (n_ja - 1 - step) * n_ka + (n_ka - dk) % n_ka
        pltpu.make_async_remote_copy(
            send.at[step * n_ka + to_k], recv.at[slot], m_s, m_r, device_id={"ja": to_j, "ka": to_k}, device_id_type=MESH).start()

    @pl.loop(0, n_ja - 1)
    def _(step):
        contract(step)
        for dk in range(n_ka):
            push(step, dk)

    contract(n_ja - 1)
    for dk in range(1, n_ka):
        push(n_ja - 1, dk)
    recv[0] = send[(n_ja - 1) * n_ka + ka]

    gc_part = gc_all.at[pl.ds(1, n_ka - 1)]
    gb_part = gb_all.at[pl.ds(1, n_ja - 1)]
    pltpu.make_async_copy(gc_part, gc_part, gc_r).wait()
    pltpu.make_async_copy(gb_part, gb_part, gb_r).wait()
    gram = jnp.sum(gc_all[...], axis=0) * jnp.sum(gb_all[...], axis=0)
    gram = jnp.concatenate([gram[:, g * rank:(g + 1) * rank] for g in range(groups)], axis=0)
    inverse = jnp.concatenate([inverse_spd(gram)] * groups, axis=0)

    m_part = recv.at[pl.ds(1, n_ja * n_ka - 1)]
    pltpu.make_async_copy(m_part, m_part, m_r).wait()
    total = jnp.sum(recv[...], axis=0)
    lane = lane_group(total.shape, rank)
    spread = jnp.concatenate([jnp.where(lane == g, total, 0.0) for g in range(groups)], axis=0)
    out_ref[...] = jnp.dot(spread, inverse, precision=HIGHEST, preferred_element_type=F32)

    pltpu.make_async_copy(fb_part, fb_part, fb_s).wait()
    pltpu.make_async_copy(gc_part, gc_part, gc_s).wait()
    pltpu.make_async_copy(gb_part, gb_part, gb_s).wait()
    pltpu.make_async_copy(m_part, m_part, m_s).wait()


def solution(mesh):
    sizes = (mesh.shape["ia"], mesh.shape["ja"], mesh.shape["ka"])
    n_ia, n_ja, n_ka = sizes

    def per_device(tensor, factor_b, factor_c):
        block_i, block_k, block_j = tensor.shape
        shard, rank = factor_b.shape
        rows = block_i // (n_ja * n_ka)
        groups = LANES // rank
        dma = pltpu.SemaphoreType.DMA
        vmem = pltpu.VMEM
        return pl.pallas_call(
            functools.partial(kernel, sizes),
            out_shape=jax.ShapeDtypeStruct((rows, rank), F32),
            in_specs=[pl.BlockSpec(memory_space=pltpu.HBM)] * 3,
            out_specs=pl.BlockSpec(memory_space=pltpu.VMEM),
            scratch_shapes=[
                vmem((block_i, block_k, block_j), BF16),
                vmem((rank, shard), F32),
                vmem((block_k, rank), F32),
                vmem((rank // 2, 2 * shard), F32),
                vmem((n_ia, rank // 2, 2 * shard), F32),
                vmem((n_ka, rank // groups, LANES), F32),
                vmem((n_ja, rank // groups, LANES), F32),
                vmem((block_j, LANES), BF16),
                vmem((n_ja * n_ka, rows // groups, LANES), F32),
                vmem((n_ja * n_ka, rows // groups, LANES), F32),
                dma((n_ja,)), dma((2,)),
                dma, dma, dma, dma, dma, dma, dma, dma,
            ],
            compiler_params=pltpu.CompilerParams(collective_id=0, has_side_effects=True, vmem_limit_bytes=56 << 20),
        )(tensor, factor_b.T, factor_c)

    return jax.shard_map(
        per_device,
        mesh=mesh,
        in_specs=(P("ia", "ka", "ja"), P(("ja", "ia"), None), P("ka", None)),
        out_specs=P(("ia", "ja", "ka"), None),
        check_vma=False,
    )
```

time: 421 us -> 26.6 us (0.06)
  blocking collectives: 281 us -> 0 us
  waiting for transfers between devices: 85 us -> 0 us
  Pallas kernels: 0 us -> 25.1 us
  other arithmetic: 20.2 us -> 0 us
  between operations: 13.5 us -> 0.01 us
  matrix products: 11 us -> 0 us
  local copies, waits for them, and re-layouts: 9.5 us -> 1.3 us
    psum x2 -> x0, blocking collectives: 263 us -> none  [the longest x1 250 us: per_device(): gram_b = lax.psum(local_b, ('ia', 'ja'))]
    unnamed x2 -> x0, waiting for transfers between devices: 85 us -> none
    pallas_call x0 -> x1, Pallas kernels: none -> 25.1 us  [per_device(): pl.pallas_call(functools.partial(kernel, sizes), out_shape=jax.ShapeDtype...]
    another operation x15 -> x0, other arithmetic: 20 us -> none  [the longest x4 6.17 us: apply_inverse(): jax.scipy.linalg.solve_triangular(lower_factor, matrix.T, lower=True)]
    all_gather x1 -> x0, blocking collectives: 18.4 us -> none  [per_device(): rows_b = lax.all_gather(factor_b, 'ia', axis=0, tiled=True)]
    dot_general x5 -> x0, matrix products: 9.13 us -> none  [the longest x1 5.91 us: per_device(): jnp.dot(tensor.reshape(block_i * block_k, block_j), q_b, preferred_elemen...]
  transfers between devices with their start and end apart: 1 -> 0, of which waited for: 1 -> 0; matrix products, arithmetic and copies ran while one was open for 2% -> 0% of each run, Pallas kernels for 0% -> 0%
where the time goes in v1:
time: 26.6 us; the launch traced here: 26.4 us
  Pallas kernels  25.1 us (94%)
  local copies, waits for them, and re-layouts  1.3 us (5%)
    pallas_call x1, Pallas kernels, per_device(): pl.pallas_call(functools.partial(kernel, sizes), out_shape=jax.ShapeDtype...  25.1 us
    unnamed x1, local copies, waits for them, and re-layouts  1.3 us

profile of v1, /device:TPU:1, one launch (start us, length us, event | category | flops | bytes accessed | tf_op | source)
XLA Modules:
  0.0 26.4 jit_solution(12615205728846094858)
XLA Ops:
  0.0 25.1 %shard_map.37 = f32[16,32]{1,0:T(8,128)} custom-call(bf16[512,16,512]{2,1,0:T(8,128)(2,1)} %tensor_ref.1, f32[32,64]{1,0:T(8,128)} %bitcast.1, f32[16,32]{1,0:T(8,128)} %fc_ref.1), custom_call_target="tpu_custom_call" | custom-call | tf_op jit(solution)/shard_map/pallas_call | solution.py:192
  25.1 1.3 %copy.5 = f32[16,32]{1,0:T(8,128)} copy(f32[16,32]{1,0:T(8,128)} %shard_map.37) | data formatting | bytes 4096

commit v2 on v1

v2 whole, which is shorter than its diff:
```python
import functools

import jax
import jax.numpy as jnp
from jax import lax
from jax.experimental import pallas as pl
from jax.experimental.pallas import tpu as pltpu
from jax.sharding import PartitionSpec as P

MESH = pl.DeviceIdType.MESH
HIGHEST = lax.Precision.HIGHEST
F32 = jnp.float32
BF16 = jnp.bfloat16
LANES = 128


def lane_group(shape, rank):
    return lax.broadcasted_iota(jnp.int32, shape, 1) // rank


def tile_lanes(x):
    return jnp.concatenate([x] * (LANES // x.shape[1]), axis=1)


def pack_rows(x, rank):
    groups = LANES // rank
    m = x.shape[0] // groups
    lane = lane_group((m, LANES), rank)
    packed = x[:m]
    for g in range(1, groups):
        packed = jnp.where(lane == g, x[g * m:(g + 1) * m], packed)
    return packed


def inverse_spd(matrix):
    n = matrix.shape[0]
    row_id = lax.broadcasted_iota(jnp.int32, (n, n), 0)
    lane_id = lax.broadcasted_iota(jnp.int32, (n, n), 1)
    lane_row = lax.broadcasted_iota(jnp.int32, (1, n), 1)
    for k in range(n):
        row = matrix[k:k + 1, :]
        col = matrix[:, k:k + 1]
        inv = 1.0 / matrix[k:k + 1, k:k + 1]
        scaled = jnp.where(lane_row == k, inv, row * inv)
        rest = jnp.where(lane_id == k, 0.0, matrix)
        matrix = jnp.where(row_id == k, scaled, rest - col * scaled)
    return matrix


def kernel(sizes, tensor_ref, fbt_ref, fc_ref, out_ref,
           tbuf, fbt_own, fc_own, fb_send, fb_all, gc_all, gb_all, weights, sums, send, recv,
           load_sem, own_sem, line_sem, plane_sem, fb_s, fb_r, gc_s, gc_r, gb_s, gb_r, m_s, m_r):
    n_ia, n_ja, n_ka = sizes
    n_plane = n_ja * n_ka
    ia, ja, ka = lax.axis_index("ia"), lax.axis_index("ja"), lax.axis_index("ka")
    place = ja * n_ka + ka
    half = n_ia // 2
    mine = ia // half
    rank, shard = fbt_own.shape
    block_k = tbuf.shape[1]
    rows = out_ref.shape[0]
    group_rows = rows * n_ka
    groups = LANES // rank
    depth = half * shard

    def up(index, by, size):
        return lax.rem(index + by, size)

    def in_line(z):
        return {"ia": z}

    def in_plane(p):
        return {"ja": p // n_ka, "ka": p % n_ka}

    own_b = pltpu.make_async_copy(fbt_ref, fbt_own, own_sem.at[0])
    own_c = pltpu.make_async_copy(fc_ref, fc_own, own_sem.at[1])
    own_b.start()
    own_c.start()

    barrier = pltpu.get_barrier_semaphore()

    @pl.loop(ia + 1, n_ia)
    def _(z):
        pl.semaphore_signal(barrier, inc=1, device_id=in_line(z), device_id_type=MESH)

    @pl.loop(place + 1, n_plane)
    def _(p):
        pl.semaphore_signal(barrier, inc=1, device_id=in_plane(p), device_id_type=MESH)

    def load(step):
        part = pl.ds(step * group_rows, group_rows)
        return pltpu.make_async_copy(tensor_ref.at[part], tbuf.at[part], load_sem.at[step])

    @pl.loop(0, n_ja)
    def _(step):
        load(step).start()

    own_b.wait()
    own_c.wait()
    packed_rows = rank // 2
    own = fbt_own[...]
    packed_b = jnp.concatenate([own[:packed_rows], own[packed_rows:]], axis=1)
    fb_send[...] = packed_b
    fb_all[ia] = packed_b
    fc_tiled = tile_lanes(fc_own[...])
    gc_all[0] = pack_rows(
        lax.dot_general(fc_own[...], fc_tiled, (((0,), (0,)), ((), ())), precision=HIGHEST, preferred_element_type=F32), rank)

    def push_rows(z):
        pltpu.make_async_remote_copy(
            fb_send, fb_all.at[ia], fb_s, fb_r.at[mine], device_id=in_line(z), device_id_type=MESH).start()

    def answer_rows(z):
        pl.semaphore_wait(line_sem.at[z], 1)
        push_rows(z)

    @pl.when(ia + place > 0)
    def _():
        pl.semaphore_wait(barrier, ia + place)

    pl.semaphore_signal(plane_sem, inc=1)

    @pl.loop(0, ia)
    def _(z):
        push_rows(z)

    @pl.loop(0, ia)
    def _(z):
        pl.semaphore_signal(line_sem.at[ia], inc=1, device_id=in_line(z), device_id_type=MESH)

    @pl.loop(0, place)
    def _(p):
        pl.semaphore_signal(plane_sem, inc=1, device_id=in_plane(p), device_id_type=MESH)

    pl.loop(ia + 1, (mine + 1) * half)(answer_rows)

    def await_rows(which, count):
        part = fb_all.at[pl.ds(0, count)]
        pltpu.make_async_copy(part, part, fb_r.at[which]).wait()

    def prepare(which):
        uppers, lowers = [], []
        for s in range(half):
            piece = fb_all[which * half + s]
            uppers.append(piece[:, :shard])
            lowers.append(piece[:, shard:])
        fbt = jnp.concatenate([jnp.concatenate(uppers, axis=1), jnp.concatenate(lowers, axis=1)], axis=0)
        high = fbt.astype(BF16)
        rest = fbt - high.astype(F32)
        middle = rest.astype(BF16)
        low = (rest - middle.astype(F32)).astype(BF16)
        stacked = jnp.concatenate([high.astype(F32), middle.astype(F32), low.astype(F32), jnp.zeros_like(fbt)], axis=0)
        weights[...] = stacked.T.astype(BF16)
        gram = lax.dot_general(fbt, jnp.concatenate([fbt] * groups, axis=0), (((1,), (1,)), ((), ())),
                               precision=HIGHEST, preferred_element_type=F32)
        return pack_rows(gram, rank)

    def contract(step, which):
        columns = pl.ds(pl.multiple_of(which * depth, depth), depth)
        x = tbuf[pl.ds(step * group_rows, group_rows), :, columns].reshape(group_rows * block_k, depth)
        flat = jnp.dot(x, weights[...], preferred_element_type=F32).reshape(group_rows, block_k, LANES)
        return jnp.sum(flat * fc_tiled[None], axis=1)

    pl.loop(half + mine * half, n_ia)(answer_rows)
    await_rows(mine, half - 1)
    gb_all[0] = prepare(mine)

    @pl.loop(0, n_ja)
    def _(step):
        load(step).wait()

    @pl.loop(0, n_ja, unroll=n_ja)
    def _(step):
        sums[step] = contract(step, mine)

    pl.semaphore_wait(plane_sem, n_plane - place)

    @pl.loop(1, n_ka)
    def _(d):
        pltpu.make_async_remote_copy(gc_all.at[0], gc_all.at[n_ka - d], gc_s, gc_r, device_id={"ka": up(ka, d, n_ka)}, device_id_type=MESH).start()

    await_rows(1 - mine, half)
    gb_all[0] = gb_all[0] + prepare(1 - mine)

    @pl.loop(1, n_ja)
    def _(d):
        pltpu.make_async_remote_copy(gb_all.at[0], gb_all.at[n_ja - d], gb_s, gb_r, device_id={"ja": up(ja, d, n_ja)}, device_id_type=MESH).start()

    def finish(step):
        part = sums[step] + contract(step, 1 - mine)
        part = part + pltpu.roll(part, 2 * rank, 1)
        part = part + pltpu.roll(part, rank, 1)
        for b in range(n_ka):
            send[step * n_ka + b] = pack_rows(part[b * rows:(b + 1) * rows], rank)

    pl.loop(0, n_ja, unroll=n_ja)(finish)
    for dj in sorted(range(n_ja), key=lambda d: -min(d, n_ja - d)):
        for dk in sorted(range(n_ka), key=lambda d: -min(d, n_ka - d)):
            if dj or dk:
                to_j, to_k = up(ja, dj, n_ja), up(ka, dk, n_ka)
                slot = (n_ja - dj) % n_ja * n_ka + (n_ka - dk) % n_ka
                pltpu.make_async_remote_copy(
                    send.at[to_j * n_ka + to_k], recv.at[slot], m_s, m_r,
                    device_id={"ja": to_j, "ka": to_k}, device_id_type=MESH).start()
    recv[0] = send[place]

    gc_part = gc_all.at[pl.ds(1, n_ka - 1)]
    gb_part = gb_all.at[pl.ds(1, n_ja - 1)]
    pltpu.make_async_copy(gc_part, gc_part, gc_r).wait()
    pltpu.make_async_copy(gb_part, gb_part, gb_r).wait()
    gram = jnp.sum(gc_all[...], axis=0) * jnp.sum(gb_all[...], axis=0)
    gram = jnp.concatenate([gram[:, g * rank:(g + 1) * rank] for g in range(groups)], axis=0)
    inverse = jnp.concatenate([inverse_spd(gram)] * groups, axis=0)

    fb_part = fb_all.at[pl.ds(0, n_ia - 1)]
    pltpu.make_async_copy(fb_part, fb_part, fb_s).wait()
    pltpu.make_async_copy(gc_part, gc_part, gc_s).wait()
    pltpu.make_async_copy(gb_part, gb_part, gb_s).wait()
    m_part = recv.at[pl.ds(1, n_plane - 1)]
    pltpu.make_async_copy(m_part, m_part, m_s).wait()
    pltpu.make_async_copy(m_part, m_part, m_r).wait()
    total = jnp.sum(recv[...], axis=0)
    lane = lane_group(total.shape, rank)
    spread = jnp.concatenate([jnp.where(lane == g, total, 0.0) for g in range(groups)], axis=0)
    out_ref[...] = jnp.dot(spread, inverse, precision=HIGHEST, preferred_element_type=F32)


def solution(mesh):
    sizes = (mesh.shape["ia"], mesh.shape["ja"], mesh.shape["ka"])
    n_ia, n_ja, n_ka = sizes

    def per_device(tensor, factor_b, factor_c):
        block_i, block_k, block_j = tensor.shape
        shard, rank = factor_b.shape
        rows = block_i // (n_ja * n_ka)
        groups = LANES // rank
        dma = pltpu.SemaphoreType.DMA
        vmem = pltpu.VMEM
        return pl.pallas_call(
            functools.partial(kernel, sizes),
            out_shape=pltpu.VMEM((rows, rank), F32),
            in_specs=[pl.BlockSpec(memory_space=pltpu.HBM)] * 3,
            out_specs=pl.BlockSpec(memory_space=pltpu.VMEM),
            scratch_shapes=[
                vmem((block_i, block_k, block_j), BF16),
                vmem((rank, shard), F32),
                vmem((block_k, rank), F32),
                vmem((rank // 2, 2 * shard), F32),
                vmem((n_ia, rank // 2, 2 * shard), F32),
                vmem((n_ka, rank // groups, LANES), F32),
                vmem((n_ja, rank // groups, LANES), F32),
                vmem((block_j // 2, LANES), BF16),
                vmem((n_ja, rows * n_ka, LANES), F32),
                vmem((n_ja * n_ka, rows // groups, LANES), F32),
                vmem((n_ja * n_ka, rows // groups, LANES), F32),
                dma((n_ja,)), dma((2,)),
                pltpu.SemaphoreType.REGULAR((n_ia,)), pltpu.SemaphoreType.REGULAR,
                dma, dma((2,)), dma, dma, dma, dma, dma, dma,
            ],
            compiler_params=pltpu.CompilerParams(collective_id=0, has_side_effects=True, vmem_limit_bytes=56 << 20),
        )(tensor, factor_b.T, factor_c)

    return jax.shard_map(
        per_device,
        mesh=mesh,
        in_specs=(P("ia", "ka", "ja"), P(("ja", "ia"), None), P("ka", None)),
        out_specs=P(("ia", "ja", "ka"), None),
        check_vma=False,
    )
```

time: 26.6 us -> 22.9 us (0.86)
  Pallas kernels: 25.1 us -> 22.1 us
  local copies, waits for them, and re-layouts: 1.3 us -> 0.6 us
    pallas_call x1, Pallas kernels: 25.1 us -> 22.1 us  [per_device(): pl.pallas_call(functools.partial(kernel, sizes), out_shape=pltpu.VMEM((ro...]
    unnamed x1, local copies, waits for them, and re-layouts: 1.3 us -> 0.6 us
where the time goes in v2:
time: 22.9 us; the launch traced here: 22.7 us
  Pallas kernels  22.1 us (97%)
  local copies, waits for them, and re-layouts  0.6 us (3%)
    pallas_call x1, Pallas kernels, per_device(): pl.pallas_call(functools.partial(kernel, sizes), out_shape=pltpu.VMEM((ro...  22.1 us
    unnamed x1, local copies, waits for them, and re-layouts  0.6 us

profile of v2, /device:TPU:1, one launch (start us, length us, event | category | flops | bytes accessed | tf_op | source)
XLA Modules:
  0.0 22.7 jit_solution(6607452195141860751)
XLA Ops:
  0.0 22.1 %shard_map.37 = f32[16,32]{1,0:T(8,128)S(1)} custom-call(bf16[512,16,512]{2,1,0:T(8,128)(2,1)} %tensor_ref.1, f32[32,64]{1,0:T(8,128)} %bitcast.1, f32[16,32]{1,0:T(8,128)} %fc_ref.1), custom_call_target="tpu_custom_call" | custom-call | tf_op jit(solution)/shard_map/pallas_call | solution.py:239
  22.1 0.6 %copy.5 = f32[16,32]{1,0:T(8,128)} copy(f32[16,32]{1,0:T(8,128)S(1)} %shard_map.37) | data formatting | bytes 4096

commit v3 on v2

--- a/solution.py
+++ b/solution.py
@@ -32,18 +32,22 @@
     return packed
 
 
-def inverse_spd(matrix):
+def inverse_spd(matrix, block=8):
     n = matrix.shape[0]
     row_id = lax.broadcasted_iota(jnp.int32, (n, n), 0)
     lane_id = lax.broadcasted_iota(jnp.int32, (n, n), 1)
     lane_row = lax.broadcasted_iota(jnp.int32, (1, n), 1)
-    for k in range(n):
-        row = matrix[k:k + 1, :]
-        col = matrix[:, k:k + 1]
-        inv = 1.0 / matrix[k:k + 1, k:k + 1]
-        scaled = jnp.where(lane_row == k, inv, row * inv)
-        rest = jnp.where(lane_id == k, 0.0, matrix)
-        matrix = jnp.where(row_id == k, scaled, rest - col * scaled)
+    for start in range(0, n, block):
+        spread = {j: jnp.broadcast_to(matrix[:, j:j + 1], (n, n)) for j in range(start, start + block)}
+        for k in range(start, start + block):
+            col = spread[k]
+            inv = 1.0 / col[k:k + 1, :]
+            scaled = jnp.where(lane_row == k, inv, matrix[k:k + 1, :] * inv)
+            rest = jnp.where(lane_id == k, 0.0, matrix)
+            matrix = jnp.where(row_id == k, scaled, rest - col * scaled)
+            for j in range(k + 1, start + block):
+                pivot_row = spread[j][k:k + 1, :] * inv
+                spread[j] = jnp.where(row_id == k, pivot_row, spread[j] - col * pivot_row)
     return matrix
 
 
@@ -88,7 +92,7 @@
         pl.semaphore_signal(barrier, inc=1, device_id=in_plane(p), device_id_type=MESH)
 
     def load(step):
-        part = pl.ds(step * group_rows, group_rows)
+        part = pl.ds(pl.multiple_of(step * group_rows, group_rows), group_rows)
         return pltpu.make_async_copy(tensor_ref.at[part], tbuf.at[part], load_sem.at[step])
 
     @pl.loop(0, n_ja)
@@ -96,15 +100,11 @@
         load(step).start()
 
     own_b.wait()
-    own_c.wait()
     packed_rows = rank // 2
     own = fbt_own[...]
     packed_b = jnp.concatenate([own[:packed_rows], own[packed_rows:]], axis=1)
     fb_send[...] = packed_b
     fb_all[ia] = packed_b
-    fc_tiled = tile_lanes(fc_own[...])
-    gc_all[0] = pack_rows(
-        lax.dot_general(fc_own[...], fc_tiled, (((0,), (0,)), ((), ())), precision=HIGHEST, preferred_element_type=F32), rank)
 
     def push_rows(z):
         pltpu.make_async_remote_copy(
@@ -157,10 +157,14 @@
 
     def contract(step, which):
         columns = pl.ds(pl.multiple_of(which * depth, depth), depth)
-        x = tbuf[pl.ds(step * group_rows, group_rows), :, columns].reshape(group_rows * block_k, depth)
+        x = tbuf[pl.ds(pl.multiple_of(step * group_rows, group_rows), group_rows), :, columns].reshape(group_rows * block_k, depth)
         flat = jnp.dot(x, weights[...], preferred_element_type=F32).reshape(group_rows, block_k, LANES)
         return jnp.sum(flat * fc_tiled[None], axis=1)
 
+    own_c.wait()
+    fc_tiled = tile_lanes(fc_own[...])
+    gc_all[0] = pack_rows(
+        lax.dot_general(fc_own[...], fc_tiled, (((0,), (0,)), ((), ())), precision=HIGHEST, preferred_element_type=F32), rank)
     pl.loop(half + mine * half, n_ia)(answer_rows)
     await_rows(mine, half - 1)
     gb_all[0] = prepare(mine)
@@ -186,23 +190,30 @@
     def _(d):
         pltpu.make_async_remote_copy(gb_all.at[0], gb_all.at[n_ja - d], gb_s, gb_r, device_id={"ja": up(ja, d, n_ja)}, device_id_type=MESH).start()
 
-    def finish(step):
+    def finish(dj):
+        step = up(ja, dj, n_ja)
         part = sums[step] + contract(step, 1 - mine)
         part = part + pltpu.roll(part, 2 * rank, 1)
         part = part + pltpu.roll(part, rank, 1)
         for b in range(n_ka):
-            send[step * n_ka + b] = pack_rows(part[b * rows:(b + 1) * rows], rank)
-
-    pl.loop(0, n_ja, unroll=n_ja)(finish)
-    for dj in sorted(range(n_ja), key=lambda d: -min(d, n_ja - d)):
+            send[dj * n_ka + b] = pack_rows(part[b * rows:(b + 1) * rows], rank)
+
+    def push(dj, dk):
+        to_j, to_k = up(ja, dj, n_ja), up(ka, dk, n_ka)
+        slot = (n_ja - dj) % n_ja * n_ka + (n_ka - dk) % n_ka
+        pltpu.make_async_remote_copy(
+            send.at[dj * n_ka + to_k], recv.at[slot], m_s, m_r, device_id={"ja": to_j, "ka": to_k}, device_id_type=MESH).start()
+
+    order = sorted(range(n_ja), key=lambda d: -min(d, n_ja - d))
+    batch = n_ja // 4
+    for first in range(0, n_ja, batch):
+        for dj in order[first:first + batch]:
+            finish(dj)
         for dk in sorted(range(n_ka), key=lambda d: -min(d, n_ka - d)):
-            if dj or dk:
-                to_j, to_k = up(ja, dj, n_ja), up(ka, dk, n_ka)
-                slot = (n_ja - dj) % n_ja * n_ka + (n_ka - dk) % n_ka
-                pltpu.make_async_remote_copy(
-                    send.at[to_j * n_ka + to_k], recv.at[slot], m_s, m_r,
-                    device_id={"ja": to_j, "ka": to_k}, device_id_type=MESH).start()
-    recv[0] = send[place]
+            for dj in order[first:first + batch]:
+                if dj or dk:
+                    push(dj, dk)
+    recv[0] = send[ka]
 
     gc_part = gc_all.at[pl.ds(1, n_ka - 1)]
     gb_part = gb_all.at[pl.ds(1, n_ja - 1)]

time: 22.9 us -> 21.4 us (0.934)
  Pallas kernels: 22.1 us -> 20.6 us
    pallas_call x1, Pallas kernels: 22.1 us -> 20.6 us  [per_device(): pl.pallas_call(functools.partial(kernel, sizes), out_shape=pltpu.VMEM((ro...]
where the time goes in v3:
time: 21.4 us; the launch traced here: 21.3 us
  Pallas kernels  20.6 us (96%)
  local copies, waits for them, and re-layouts  0.6 us (3%)
    pallas_call x1, Pallas kernels, per_device(): pl.pallas_call(functools.partial(kernel, sizes), out_shape=pltpu.VMEM((ro...  20.6 us
    unnamed x1, local copies, waits for them, and re-layouts  0.6 us

profile of v3, /device:TPU:1, one launch (start us, length us, event | category | flops | bytes accessed | tf_op | source)
XLA Modules:
  0.0 21.3 jit_solution(3952809219752477656)
XLA Ops:
  0.0 20.6 %shard_map.37 = f32[16,32]{1,0:T(8,128)S(1)} custom-call(bf16[512,16,512]{2,1,0:T(8,128)(2,1)} %tensor_ref.1, f32[32,64]{1,0:T(8,128)} %bitcast.1, f32[16,32]{1,0:T(8,128)} %fc_ref.1), custom_call_target="tpu_custom_call" | custom-call | tf_op jit(solution)/shard_map/pallas_call | solution.py:250
  20.7 0.6 %copy.5 = f32[16,32]{1,0:T(8,128)} copy(f32[16,32]{1,0:T(8,128)S(1)} %shard_map.37) | data formatting | bytes 4096

commit v4 on v3

--- a/solution.py
+++ b/solution.py
@@ -53,7 +53,7 @@
 
 def kernel(sizes, tensor_ref, fbt_ref, fc_ref, out_ref,
            tbuf, fbt_own, fc_own, fb_send, fb_all, gc_all, gb_all, weights, sums, send, recv,
-           load_sem, own_sem, line_sem, plane_sem, fb_s, fb_r, gc_s, gc_r, gb_s, gb_r, m_s, m_r):
+           load_sem, own_sem, line_sem, plane_sem, near_sem, far_sem, fb_s, fb_r, gc_s, gc_r, gb_s, gb_r, m_s, m_r):
     n_ia, n_ja, n_ka = sizes
     n_plane = n_ja * n_ka
     ia, ja, ka = lax.axis_index("ia"), lax.axis_index("ja"), lax.axis_index("ka")
@@ -87,9 +87,11 @@
     def _(z):
         pl.semaphore_signal(barrier, inc=1, device_id=in_line(z), device_id_type=MESH)
 
-    @pl.loop(place + 1, n_plane)
-    def _(p):
-        pl.semaphore_signal(barrier, inc=1, device_id=in_plane(p), device_id_type=MESH)
+    @pl.when(ia == 0)
+    def _():
+        @pl.loop(place + 1, n_plane)
+        def _(p):
+            pl.semaphore_signal(barrier, inc=1, device_id=in_plane(p), device_id_type=MESH)
 
     def load(step):
         part = pl.ds(pl.multiple_of(step * group_rows, group_rows), group_rows)
@@ -114,11 +116,13 @@
         pl.semaphore_wait(line_sem.at[z], 1)
         push_rows(z)
 
-    @pl.when(ia + place > 0)
-    def _():
-        pl.semaphore_wait(barrier, ia + place)
-
-    pl.semaphore_signal(plane_sem, inc=1)
+    @pl.when(ia > 0)
+    def _():
+        pl.semaphore_wait(barrier, ia)
+
+    @pl.when((ia == 0) & (place > 0))
+    def _():
+        pl.semaphore_wait(barrier, place)
 
     @pl.loop(0, ia)
     def _(z):
@@ -128,9 +132,13 @@
     def _(z):
         pl.semaphore_signal(line_sem.at[ia], inc=1, device_id=in_line(z), device_id_type=MESH)
 
-    @pl.loop(0, place)
-    def _(p):
-        pl.semaphore_signal(plane_sem, inc=1, device_id=in_plane(p), device_id_type=MESH)
+    @pl.when(ia == 0)
+    def _():
+        pl.semaphore_signal(plane_sem, inc=1)
+
+        @pl.loop(0, place)
+        def _(p):
+            pl.semaphore_signal(plane_sem, inc=1, device_id=in_plane(p), device_id_type=MESH)
 
     pl.loop(ia + 1, (mine + 1) * half)(answer_rows)
 
@@ -165,7 +173,21 @@
     fc_tiled = tile_lanes(fc_own[...])
     gc_all[0] = pack_rows(
         lax.dot_general(fc_own[...], fc_tiled, (((0,), (0,)), ((), ())), precision=HIGHEST, preferred_element_type=F32), rank)
-    pl.loop(half + mine * half, n_ia)(answer_rows)
+    @pl.when(ia == 0)
+    def _():
+        pl.semaphore_wait(plane_sem, n_plane - place)
+
+        @pl.loop(1, n_plane)
+        def _(d):
+            pl.semaphore_signal(near_sem, inc=1, device_id=in_plane(lax.rem(place + d, n_plane)), device_id_type=MESH)
+
+    answer_first = ia == half - 1
+    answer_later = ia < half - 1
+
+    def answer_far():
+        pl.loop(half, n_ia)(answer_rows)
+
+    pl.when(answer_first)(answer_far)
     await_rows(mine, half - 1)
     gb_all[0] = prepare(mine)
 
@@ -177,14 +199,41 @@
     def _(step):
         sums[step] = contract(step, mine)
 
-    pl.semaphore_wait(plane_sem, n_plane - place)
+    pl.when(answer_later)(answer_far)
+
+    def tell(first, end):
+        @pl.loop(first, end)
+        def _(z):
+            pl.semaphore_signal(plane_sem, inc=1, device_id=in_line(z), device_id_type=MESH)
+
+    @pl.when(ia == 0)
+    def _():
+        @pl.loop(1, n_ka)
+        def _(d):
+            pl.semaphore_signal(far_sem.at[0], inc=1, device_id={"ka": up(ka, d, n_ka)}, device_id_type=MESH)
+
+        pl.semaphore_wait(near_sem, n_plane - 1)
+        tell(1, half)
+
+    await_rows(1 - mine, half)
+
+    @pl.when(ia == 0)
+    def _():
+        pl.semaphore_wait(far_sem.at[0], n_ka - 1)
+
+        @pl.loop(1, n_ja)
+        def _(d):
+            pl.semaphore_signal(far_sem.at[1], inc=1, device_id={"ja": up(ja, d, n_ja)}, device_id_type=MESH)
+
+    gb_all[0] = gb_all[0] + prepare(1 - mine)
+
+    @pl.when(ia > 0)
+    def _():
+        pl.semaphore_wait(plane_sem, 1)
 
     @pl.loop(1, n_ka)
     def _(d):
         pltpu.make_async_remote_copy(gc_all.at[0], gc_all.at[n_ka - d], gc_s, gc_r, device_id={"ka": up(ka, d, n_ka)}, device_id_type=MESH).start()
-
-    await_rows(1 - mine, half)
-    gb_all[0] = gb_all[0] + prepare(1 - mine)
 
     @pl.loop(1, n_ja)
     def _(d):
@@ -205,7 +254,7 @@
             send.at[dj * n_ka + to_k], recv.at[slot], m_s, m_r, device_id={"ja": to_j, "ka": to_k}, device_id_type=MESH).start()
 
     order = sorted(range(n_ja), key=lambda d: -min(d, n_ja - d))
-    batch = n_ja // 4
+    batch = max(1, n_ja // 2)
     for first in range(0, n_ja, batch):
         for dj in order[first:first + batch]:
             finish(dj)
@@ -214,6 +263,12 @@
                 if dj or dk:
                     push(dj, dk)
     recv[0] = send[ka]
+
+    @pl.when(ia == 0)
+    def _():
+        pl.semaphore_wait(far_sem.at[1], n_ja - 1)
+        tell(half, n_ia)
+
 
     gc_part = gc_all.at[pl.ds(1, n_ka - 1)]
     gb_part = gb_all.at[pl.ds(1, n_ja - 1)]
@@ -265,7 +320,7 @@
                 vmem((n_ja * n_ka, rows // groups, LANES), F32),
                 vmem((n_ja * n_ka, rows // groups, LANES), F32),
                 dma((n_ja,)), dma((2,)),
-                pltpu.SemaphoreType.REGULAR((n_ia,)), pltpu.SemaphoreType.REGULAR,
+                pltpu.SemaphoreType.REGULAR((n_ia,)), pltpu.SemaphoreType.REGULAR, pltpu.SemaphoreType.REGULAR, pltpu.SemaphoreType.REGULAR((2,)),
                 dma, dma((2,)), dma, dma, dma, dma, dma, dma,
             ],
             compiler_params=pltpu.CompilerParams(collective_id=0, has_side_effects=True, vmem_limit_bytes=56 << 20),

time: 21.4 us -> 20.9 us (0.977)
  Pallas kernels: 20.6 us -> 20.1 us
    pallas_call x1, Pallas kernels: 20.6 us -> 20.1 us  [per_device(): pl.pallas_call(functools.partial(kernel, sizes), out_shape=pltpu.VMEM((ro...]
where the time goes in v4:
time: 20.9 us; the launch traced here: 20.7 us
  Pallas kernels  20.1 us (96%)
  local copies, waits for them, and re-layouts  0.6 us (3%)
    pallas_call x1, Pallas kernels, per_device(): pl.pallas_call(functools.partial(kernel, sizes), out_shape=pltpu.VMEM((ro...  20.1 us
    unnamed x1, local copies, waits for them, and re-layouts  0.6 us

profile of v4, /device:TPU:1, one launch (start us, length us, event | category | flops | bytes accessed | tf_op | source)
XLA Modules:
  0.0 20.7 jit_solution(16358728402568269203)
XLA Ops:
  0.0 20.1 %shard_map.37 = f32[16,32]{1,0:T(8,128)S(1)} custom-call(bf16[512,16,512]{2,1,0:T(8,128)(2,1)} %tensor_ref.1, f32[32,64]{1,0:T(8,128)} %bitcast.1, f32[16,32]{1,0:T(8,128)} %fc_ref.1), custom_call_target="tpu_custom_call" | custom-call | tf_op jit(solution)/shard_map/pallas_call | solution.py:305
  20.1 0.6 %copy.5 = f32[16,32]{1,0:T(8,128)} copy(f32[16,32]{1,0:T(8,128)S(1)} %shard_map.37) | data formatting | bytes 4096

commit v5 on v4

--- a/solution.py
+++ b/solution.py
@@ -159,6 +159,9 @@
         low = (rest - middle.astype(F32)).astype(BF16)
         stacked = jnp.concatenate([high.astype(F32), middle.astype(F32), low.astype(F32), jnp.zeros_like(fbt)], axis=0)
         weights[...] = stacked.T.astype(BF16)
+        return fbt
+
+    def gram_rows(fbt):
         gram = lax.dot_general(fbt, jnp.concatenate([fbt] * groups, axis=0), (((1,), (1,)), ((), ())),
                                precision=HIGHEST, preferred_element_type=F32)
         return pack_rows(gram, rank)
@@ -181,15 +184,16 @@
         def _(d):
             pl.semaphore_signal(near_sem, inc=1, device_id=in_plane(lax.rem(place + d, n_plane)), device_id_type=MESH)
 
-    answer_first = ia == half - 1
-    answer_later = ia < half - 1
-
-    def answer_far():
-        pl.loop(half, n_ia)(answer_rows)
-
-    pl.when(answer_first)(answer_far)
+    pl.loop(half + mine * half, n_ia)(answer_rows)
+
+    @pl.when(ia == 0)
+    def _():
+        @pl.loop(1, n_ka)
+        def _(d):
+            pl.semaphore_signal(far_sem.at[0], inc=1, device_id={"ka": up(ka, d, n_ka)}, device_id_type=MESH)
+
     await_rows(mine, half - 1)
-    gb_all[0] = prepare(mine)
+    gb_all[0] = gram_rows(prepare(mine))
 
     @pl.loop(0, n_ja)
     def _(step):
@@ -198,8 +202,6 @@
     @pl.loop(0, n_ja, unroll=n_ja)
     def _(step):
         sums[step] = contract(step, mine)
-
-    pl.when(answer_later)(answer_far)
 
     def tell(first, end):
         @pl.loop(first, end)
@@ -208,67 +210,72 @@
 
     @pl.when(ia == 0)
     def _():
-        @pl.loop(1, n_ka)
-        def _(d):
-            pl.semaphore_signal(far_sem.at[0], inc=1, device_id={"ka": up(ka, d, n_ka)}, device_id_type=MESH)
-
         pl.semaphore_wait(near_sem, n_plane - 1)
         tell(1, half)
 
+    @pl.when(ia == 0)
+    def _():
+        pl.semaphore_wait(far_sem.at[0], n_ka - 1)
+
+        @pl.loop(1, n_ja)
+        def _(d):
+            pl.semaphore_signal(far_sem.at[1], inc=1, device_id={"ja": up(ja, d, n_ja)}, device_id_type=MESH)
+
     await_rows(1 - mine, half)
 
-    @pl.when(ia == 0)
-    def _():
-        pl.semaphore_wait(far_sem.at[0], n_ka - 1)
+    fbt = prepare(1 - mine)
+
+    def push_grams():
+        gb_all[0] = gb_all[0] + gram_rows(fbt)
 
         @pl.loop(1, n_ja)
         def _(d):
-            pl.semaphore_signal(far_sem.at[1], inc=1, device_id={"ja": up(ja, d, n_ja)}, device_id_type=MESH)
-
-    gb_all[0] = gb_all[0] + prepare(1 - mine)
-
-    @pl.when(ia > 0)
-    def _():
-        pl.semaphore_wait(plane_sem, 1)
-
-    @pl.loop(1, n_ka)
-    def _(d):
-        pltpu.make_async_remote_copy(gc_all.at[0], gc_all.at[n_ka - d], gc_s, gc_r, device_id={"ka": up(ka, d, n_ka)}, device_id_type=MESH).start()
-
-    @pl.loop(1, n_ja)
-    def _(d):
-        pltpu.make_async_remote_copy(gb_all.at[0], gb_all.at[n_ja - d], gb_s, gb_r, device_id={"ja": up(ja, d, n_ja)}, device_id_type=MESH).start()
-
-    def finish(dj):
-        step = up(ja, dj, n_ja)
+            pltpu.make_async_remote_copy(
+                gb_all.at[0], gb_all.at[n_ja - d], gb_s, gb_r, device_id={"ja": up(ja, d, n_ja)}, device_id_type=MESH).start()
+
+        @pl.loop(1, n_ka)
+        def _(d):
+            pltpu.make_async_remote_copy(
+                gc_all.at[0], gc_all.at[n_ka - d], gc_s, gc_r, device_id={"ka": up(ka, d, n_ka)}, device_id_type=MESH).start()
+
+    def finish(step):
         part = sums[step] + contract(step, 1 - mine)
         part = part + pltpu.roll(part, 2 * rank, 1)
         part = part + pltpu.roll(part, rank, 1)
         for b in range(n_ka):
-            send[dj * n_ka + b] = pack_rows(part[b * rows:(b + 1) * rows], rank)
-
-    def push(dj, dk):
-        to_j, to_k = up(ja, dj, n_ja), up(ka, dk, n_ka)
-        slot = (n_ja - dj) % n_ja * n_ka + (n_ka - dk) % n_ka
+            send[step * n_ka + b] = pack_rows(part[b * rows:(b + 1) * rows], rank)
+
+    def push(to_j, to_k):
         pltpu.make_async_remote_copy(
-            send.at[dj * n_ka + to_k], recv.at[slot], m_s, m_r, device_id={"ja": to_j, "ka": to_k}, device_id_type=MESH).start()
-
-    order = sorted(range(n_ja), key=lambda d: -min(d, n_ja - d))
-    batch = max(1, n_ja // 2)
-    for first in range(0, n_ja, batch):
-        for dj in order[first:first + batch]:
-            finish(dj)
-        for dk in sorted(range(n_ka), key=lambda d: -min(d, n_ka - d)):
-            for dj in order[first:first + batch]:
-                if dj or dk:
-                    push(dj, dk)
-    recv[0] = send[ka]
-
-    @pl.when(ia == 0)
-    def _():
+            send.at[to_j * n_ka + to_k], recv.at[place], m_s, m_r, device_id={"ja": to_j, "ka": to_k}, device_id_type=MESH).start()
+
+    def tell_upper():
         pl.semaphore_wait(far_sem.at[1], n_ja - 1)
         tell(half, n_ia)
 
+    far_first = sorted(range(n_ja), key=lambda d: -min(d, n_ja - d))
+    leading = [1, 0] + [d for d in far_first if d > 1]
+    upper = (ia + n_ia - 1) // n_ia
+    targets = [(1 - upper) * g + upper * up(ja, d, n_ja) for g, d in zip(leading, far_first)]
+    far_k = sorted(range(1, n_ka), key=lambda d: -min(d, n_ka - d))
+    done = 0
+    for size in (1, 3, n_ja - 4):
+        part = targets[done:done + size]
+        for to_j in part:
+            finish(to_j)
+        if done == 0:
+            pl.when(ia > 0)(functools.partial(pl.semaphore_wait, plane_sem, 1))
+        for dk in far_k:
+            for to_j in part:
+                push(to_j, up(ka, dk, n_ka))
+        for to_j in part:
+            pl.when(to_j != ja)(functools.partial(push, to_j, ka))
+        if done == 0:
+            push_grams()
+        done += size
+        if done == 4:
+            pl.when(ia == 0)(tell_upper)
+    recv[place] = send[place]
 
     gc_part = gc_all.at[pl.ds(1, n_ka - 1)]
     gb_part = gb_all.at[pl.ds(1, n_ja - 1)]
@@ -282,7 +289,7 @@
     pltpu.make_async_copy(fb_part, fb_part, fb_s).wait()
     pltpu.make_async_copy(gc_part, gc_part, gc_s).wait()
     pltpu.make_async_copy(gb_part, gb_part, gb_s).wait()
-    m_part = recv.at[pl.ds(1, n_plane - 1)]
+    m_part = recv.at[pl.ds(0, n_plane - 1)]
     pltpu.make_async_copy(m_part, m_part, m_s).wait()
     pltpu.make_async_copy(m_part, m_part, m_r).wait()
     total = jnp.sum(recv[...], axis=0)

time: 20.9 us -> 20.4 us (0.976)
  Pallas kernels: 20.1 us -> 19.4 us
    pallas_call x1, Pallas kernels: 20.1 us -> 19.4 us  [per_device(): pl.pallas_call(functools.partial(kernel, sizes), out_shape=pltpu.VMEM((ro...]
where the time goes in v5:
time: 20.4 us; the launch traced here: 20 us
  Pallas kernels  19.4 us (95%)
  local copies, waits for them, and re-layouts  0.6 us (3%)
    pallas_call x1, Pallas kernels, per_device(): pl.pallas_call(functools.partial(kernel, sizes), out_shape=pltpu.VMEM((ro...  19.4 us
    unnamed x1, local copies, waits for them, and re-layouts  0.6 us

profile of v5, /device:TPU:1, one launch (start us, length us, event | category | flops | bytes accessed | tf_op | source)
XLA Modules:
  0.0 20.0 jit_solution(17137729390038574801)
XLA Ops:
  0.0 19.4 %shard_map.37 = f32[16,32]{1,0:T(8,128)S(1)} custom-call(bf16[512,16,512]{2,1,0:T(8,128)(2,1)} %tensor_ref.1, f32[32,64]{1,0:T(8,128)} %bitcast.1, f32[16,32]{1,0:T(8,128)} %fc_ref.1), custom_call_target="tpu_custom_call" | custom-call | tf_op jit(solution)/shard_map/pallas_call | solution.py:312
  19.4 0.6 %copy.5 = f32[16,32]{1,0:T(8,128)} copy(f32[16,32]{1,0:T(8,128)S(1)} %shard_map.37) | data formatting | bytes 4096

commit v6 on v5

--- a/solution.py
+++ b/solution.py
@@ -127,9 +127,6 @@
     @pl.loop(0, ia)
     def _(z):
         push_rows(z)
-
-    @pl.loop(0, ia)
-    def _(z):
         pl.semaphore_signal(line_sem.at[ia], inc=1, device_id=in_line(z), device_id_type=MESH)
 
     @pl.when(ia == 0)
@@ -157,8 +154,7 @@
         rest = fbt - high.astype(F32)
         middle = rest.astype(BF16)
         low = (rest - middle.astype(F32)).astype(BF16)
-        stacked = jnp.concatenate([high.astype(F32), middle.astype(F32), low.astype(F32), jnp.zeros_like(fbt)], axis=0)
-        weights[...] = stacked.T.astype(BF16)
+        weights[...] = jnp.concatenate([high, middle, low, jnp.zeros_like(high)], axis=0)
         return fbt
 
     def gram_rows(fbt):
@@ -169,7 +165,7 @@
     def contract(step, which):
         columns = pl.ds(pl.multiple_of(which * depth, depth), depth)
         x = tbuf[pl.ds(pl.multiple_of(step * group_rows, group_rows), group_rows), :, columns].reshape(group_rows * block_k, depth)
-        flat = jnp.dot(x, weights[...], preferred_element_type=F32).reshape(group_rows, block_k, LANES)
+        flat = lax.dot_general(x, weights[...], (((1,), (1,)), ((), ())), preferred_element_type=F32).reshape(group_rows, block_k, LANES)
         return jnp.sum(flat * fc_tiled[None], axis=1)
 
     own_c.wait()
@@ -253,10 +249,8 @@
         pl.semaphore_wait(far_sem.at[1], n_ja - 1)
         tell(half, n_ia)
 
-    far_first = sorted(range(n_ja), key=lambda d: -min(d, n_ja - d))
-    leading = [1, 0] + [d for d in far_first if d > 1]
-    upper = (ia + n_ia - 1) // n_ia
-    targets = [(1 - upper) * g + upper * up(ja, d, n_ja) for g, d in zip(leading, far_first)]
+    targets = sorted(range(n_ja), key=lambda g: (g // 2, 1 - g % 2))
+    targets = targets[:1] + targets[2:4] + targets[1:2] + targets[4:]
     far_k = sorted(range(1, n_ka), key=lambda d: -min(d, n_ka - d))
     done = 0
     for size in (1, 3, n_ja - 4):
@@ -322,7 +316,7 @@
                 vmem((n_ia, rank // 2, 2 * shard), F32),
                 vmem((n_ka, rank // groups, LANES), F32),
                 vmem((n_ja, rank // groups, LANES), F32),
-                vmem((block_j // 2, LANES), BF16),
+                vmem((LANES, block_j // 2), BF16),
                 vmem((n_ja, rows * n_ka, LANES), F32),
                 vmem((n_ja * n_ka, rows // groups, LANES), F32),
                 vmem((n_ja * n_ka, rows // groups, LANES), F32),

time: 20.4 us -> 20.3 us (level)
  no operation moved by 1% of the time
where the time goes in v6:
time: 20.3 us; the launch traced here: 19.9 us
  Pallas kernels  19.3 us (95%)
  local copies, waits for them, and re-layouts  0.6 us (3%)
    pallas_call x1, Pallas kernels, per_device(): pl.pallas_call(functools.partial(kernel, sizes), out_shape=pltpu.VMEM((ro...  19.3 us
    unnamed x1, local copies, waits for them, and re-layouts  0.6 us

profile of v6, /device:TPU:1, one launch (start us, length us, event | category | flops | bytes accessed | tf_op | source)
XLA Modules:
  0.0 19.9 jit_solution(17660063650091945708)
XLA Ops:
  0.0 19.3 %shard_map.37 = f32[16,32]{1,0:T(8,128)S(1)} custom-call(bf16[512,16,512]{2,1,0:T(8,128)(2,1)} %tensor_ref.1, f32[32,64]{1,0:T(8,128)} %bitcast.1, f32[16,32]{1,0:T(8,128)} %fc_ref.1), custom_call_target="tpu_custom_call" | custom-call | tf_op jit(solution)/shard_map/pallas_call | solution.py:306
  19.3 0.6 %copy.5 = f32[16,32]{1,0:T(8,128)} copy(f32[16,32]{1,0:T(8,128)S(1)} %shard_map.37) | data formatting | bytes 4096

commit v7 on v6

--- a/solution.py
+++ b/solution.py
@@ -252,23 +252,31 @@
     targets = sorted(range(n_ja), key=lambda g: (g // 2, 1 - g % 2))
     targets = targets[:1] + targets[2:4] + targets[1:2] + targets[4:]
     far_k = sorted(range(1, n_ka), key=lambda d: -min(d, n_ka - d))
-    done = 0
-    for size in (1, 3, n_ja - 4):
-        part = targets[done:done + size]
-        for to_j in part:
-            finish(to_j)
-        if done == 0:
-            pl.when(ia > 0)(functools.partial(pl.semaphore_wait, plane_sem, 1))
+    first, second, third = targets[:1], targets[1:n_ja // 2], targets[n_ja // 2:]
+
+    def push_rows_of(part):
         for dk in far_k:
             for to_j in part:
                 push(to_j, up(ka, dk, n_ka))
         for to_j in part:
             pl.when(to_j != ja)(functools.partial(push, to_j, ka))
-        if done == 0:
-            push_grams()
-        done += size
-        if done == 4:
-            pl.when(ia == 0)(tell_upper)
+
+    def open_plane():
+        pl.when(ia > 0)(functools.partial(pl.semaphore_wait, plane_sem, 1))
+        push_rows_of(first)
+        push_grams()
+
+    for to_j in first:
+        finish(to_j)
+    pl.when(mine == 0)(open_plane)
+    for to_j in second:
+        finish(to_j)
+    pl.when(mine == 1)(open_plane)
+    push_rows_of(second)
+    pl.when(ia == 0)(tell_upper)
+    for to_j in third:
+        finish(to_j)
+    push_rows_of(third)
     recv[place] = send[place]
 
     gc_part = gc_all.at[pl.ds(1, n_ka - 1)]

time: 20.3 us -> 20 us (0.985); the launches traced: 19.9 us -> 19.9 us
  no operation moved by 1% of the time
where the time goes in v7:
time: 20 us; the launch traced here: 19.9 us
  Pallas kernels  19.3 us (96%)
  local copies, waits for them, and re-layouts  0.6 us (3%)
    pallas_call x1, Pallas kernels, per_device(): pl.pallas_call(functools.partial(kernel, sizes), out_shape=pltpu.VMEM((ro...  19.3 us
    unnamed x1, local copies, waits for them, and re-layouts  0.6 us

profile of v7, /device:TPU:1, one launch (start us, length us, event | category | flops | bytes accessed | tf_op | source)
XLA Modules:
  0.0 19.9 jit_solution(1795483358564192968)
XLA Ops:
  0.0 19.3 %shard_map.37 = f32[16,32]{1,0:T(8,128)S(1)} custom-call(bf16[512,16,512]{2,1,0:T(8,128)(2,1)} %tensor_ref.1, f32[32,64]{1,0:T(8,128)} %bitcast.1, f32[16,32]{1,0:T(8,128)} %fc_ref.1), custom_call_target="tpu_custom_call" | custom-call | tf_op jit(solution)/shard_map/pallas_call | solution.py:314
  19.3 0.6 %copy.5 = f32[16,32]{1,0:T(8,128)} copy(f32[16,32]{1,0:T(8,128)S(1)} %shard_map.37) | data formatting | bytes 4096

commit v8 on v7

--- a/solution.py
+++ b/solution.py
@@ -97,10 +97,6 @@
         part = pl.ds(pl.multiple_of(step * group_rows, group_rows), group_rows)
         return pltpu.make_async_copy(tensor_ref.at[part], tbuf.at[part], load_sem.at[step])
 
-    @pl.loop(0, n_ja)
-    def _(step):
-        load(step).start()
-
     own_b.wait()
     packed_rows = rank // 2
     own = fbt_own[...]
@@ -136,6 +132,10 @@
         @pl.loop(0, place)
         def _(p):
             pl.semaphore_signal(plane_sem, inc=1, device_id=in_plane(p), device_id_type=MESH)
+
+    @pl.loop(0, n_ja)
+    def _(step):
+        load(step).start()
 
     pl.loop(ia + 1, (mine + 1) * half)(answer_rows)
 

time: 20 us -> 20 us (level)
  no operation moved by 1% of the time
where the time goes in v8:
time: 20 us; the launch traced here: 19.9 us
  Pallas kernels  19.3 us (96%)
  local copies, waits for them, and re-layouts  0.6 us (3%)
    pallas_call x1, Pallas kernels, per_device(): pl.pallas_call(functools.partial(kernel, sizes), out_shape=pltpu.VMEM((ro...  19.3 us
    unnamed x1, local copies, waits for them, and re-layouts  0.6 us

profile of v8, /device:TPU:1, one launch (start us, length us, event | category | flops | bytes accessed | tf_op | source)
XLA Modules:
  0.0 19.9 jit_solution(15877610447414242058)
XLA Ops:
  0.0 19.3 %shard_map.37 = f32[16,32]{1,0:T(8,128)S(1)} custom-call(bf16[512,16,512]{2,1,0:T(8,128)(2,1)} %tensor_ref.1, f32[32,64]{1,0:T(8,128)} %bitcast.1, f32[16,32]{1,0:T(8,128)} %fc_ref.1), custom_call_target="tpu_custom_call" | custom-call | tf_op jit(solution)/shard_map/pallas_call | solution.py:314
  19.3 0.6 %copy.5 = f32[16,32]{1,0:T(8,128)} copy(f32[16,32]{1,0:T(8,128)S(1)} %shard_map.37) | data formatting | bytes 4096

commit v9 on v8

--- a/solution.py
+++ b/solution.py
@@ -162,10 +162,11 @@
                                precision=HIGHEST, preferred_element_type=F32)
         return pack_rows(gram, rank)
 
-    def contract(step, which):
+    def contract(step, which, low=0, high=n_ka):
         columns = pl.ds(pl.multiple_of(which * depth, depth), depth)
-        x = tbuf[pl.ds(pl.multiple_of(step * group_rows, group_rows), group_rows), :, columns].reshape(group_rows * block_k, depth)
-        flat = lax.dot_general(x, weights[...], (((1,), (1,)), ((), ())), preferred_element_type=F32).reshape(group_rows, block_k, LANES)
+        count = (high - low) * rows
+        x = tbuf[pl.ds(pl.multiple_of(step * group_rows + low * rows, rows), count), :, columns].reshape(count * block_k, depth)
+        flat = lax.dot_general(x, weights[...], (((1,), (1,)), ((), ())), preferred_element_type=F32).reshape(count, block_k, LANES)
         return jnp.sum(flat * fc_tiled[None], axis=1)
 
     own_c.wait()
@@ -234,12 +235,12 @@
             pltpu.make_async_remote_copy(
                 gc_all.at[0], gc_all.at[n_ka - d], gc_s, gc_r, device_id={"ka": up(ka, d, n_ka)}, device_id_type=MESH).start()
 
-    def finish(step):
-        part = sums[step] + contract(step, 1 - mine)
+    def finish(step, low=0, high=n_ka):
+        part = sums[step, low * rows:high * rows] + contract(step, 1 - mine, low, high)
         part = part + pltpu.roll(part, 2 * rank, 1)
         part = part + pltpu.roll(part, rank, 1)
-        for b in range(n_ka):
-            send[step * n_ka + b] = pack_rows(part[b * rows:(b + 1) * rows], rank)
+        for b in range(low, high):
+            send[step * n_ka + b] = pack_rows(part[(b - low) * rows:(b - low + 1) * rows], rank)
 
     def push(to_j, to_k):
         pltpu.make_async_remote_copy(
@@ -252,7 +253,7 @@
     targets = sorted(range(n_ja), key=lambda g: (g // 2, 1 - g % 2))
     targets = targets[:1] + targets[2:4] + targets[1:2] + targets[4:]
     far_k = sorted(range(1, n_ka), key=lambda d: -min(d, n_ka - d))
-    first, second, third = targets[:1], targets[1:n_ja // 2], targets[n_ja // 2:]
+    head, second, third = targets[0], targets[1:n_ja // 2], targets[n_ja // 2:]
 
     def push_rows_of(part):
         for dk in far_k:
@@ -261,17 +262,26 @@
         for to_j in part:
             pl.when(to_j != ja)(functools.partial(push, to_j, ka))
 
+    def push_head(low, high):
+        for k in range(low, high):
+            pl.when(place != head * n_ka + k)(functools.partial(push, head, k))
+
     def open_plane():
         pl.when(ia > 0)(functools.partial(pl.semaphore_wait, plane_sem, 1))
-        push_rows_of(first)
+        push_head(0, 1)
+
+    def push_rest():
+        push_head(1, n_ka)
         push_grams()
 
-    for to_j in first:
-        finish(to_j)
+    finish(head, 0, 1)
     pl.when(mine == 0)(open_plane)
+    finish(head, 1, n_ka)
+    pl.when(mine == 0)(push_rest)
     for to_j in second:
         finish(to_j)
     pl.when(mine == 1)(open_plane)
+    pl.when(mine == 1)(push_rest)
     push_rows_of(second)
     pl.when(ia == 0)(tell_upper)
     for to_j in third:

time: 20 us -> 20.2 us (1.010)
  no operation moved by 1% of the time
where the time goes in v9:
time: 20.2 us; the launch traced here: 20.1 us
  Pallas kernels  19.5 us (97%)
  local copies, waits for them, and re-layouts  0.6 us (3%)
    pallas_call x1, Pallas kernels, per_device(): pl.pallas_call(functools.partial(kernel, sizes), out_shape=pltpu.VMEM((ro...  19.5 us
    unnamed x1, local copies, waits for them, and re-layouts  0.6 us

profile of v9, /device:TPU:1, one launch (start us, length us, event | category | flops | bytes accessed | tf_op | source)
XLA Modules:
  0.0 20.1 jit_solution(13599719752726763092)
XLA Ops:
  0.0 19.5 %shard_map.37 = f32[16,32]{1,0:T(8,128)S(1)} custom-call(bf16[512,16,512]{2,1,0:T(8,128)(2,1)} %tensor_ref.1, f32[32,64]{1,0:T(8,128)} %bitcast.1, f32[16,32]{1,0:T(8,128)} %fc_ref.1), custom_call_target="tpu_custom_call" | custom-call | tf_op jit(solution)/shard_map/pallas_call | solution.py:324
  19.5 0.6 %copy.5 = f32[16,32]{1,0:T(8,128)} copy(f32[16,32]{1,0:T(8,128)S(1)} %shard_map.37) | data formatting | bytes 4096
